TPU v7x, 32 devices: a whole 2x2x4 slice. The times are simulated.
32 devices in a mesh: groups: 2 (over y), row: 4 (over z), col: 2 (over x), depth: 2 (over core).
Axes of the slice: x: 2, y: 2, z: 4, core: 2. Of those that a mesh axis runs over, the one named last changes fastest.
Arguments:
- blocks: bfloat16 [64, 20, 64, 64], P(('groups', 'row', 'col')), parts along dimension 0, may hold values from -6 to 6
- pattern: int32 [64, 20], P(('groups', 'row', 'col')), parts along dimension 0, may hold values from 0 to 31, as said below
- owner_map: int32 [2, 64, 10, 1], P('depth', ('groups', 'row', 'col')), parts along dimension 1, may hold values from 0 to 7; in each aligned block of 40 rows (0 to 39, 40 to 79, ..., all dimensions but the last counted through in order) at most 16 rows name the same one
Outputs:
- regrouped: bfloat16 [2, 16, 8, 16, 64, 64], P('depth', ('groups', 'row', 'col')), parts along dimension 1
There are 2 independent parts, one for each index of `groups`. A program takes and returns all parts, laid end to end along the dimension named above; each array names one. Nothing has to cross between parts.
Inputs may be any that keep to these rules, and one draw needn't show every extreme that they name: `pattern`: the 20 block columns of a block row are distinct and lie within 12 block positions of the row's own index, counted around the ends. `owner_map`: within one half and one aligned block of 4 block rows, no owner is named more than 16 times.
All inputs are finite; a program needn't handle non-finite values.
Results may differ from a plain program's by a relative error of at most 0.0049.
Values may be sent and summed in bfloat16 or wider, within the bound.
A program may use at most 64 MiB of HBM per device.

v0:
```python
import math

import jax
import jax.numpy as jnp
from jax import lax
from jax.sharding import PartitionSpec as P

HOPS = 3


def passed_along(value, axis, by):
    peers = lax.axis_size(axis)
    return lax.ppermute(value, axis, [(i, (i + by) % peers) for i in range(peers)])


def product_rows(left, left_pattern, local_index, near_blocks, near_pattern, first_slot, slot_span):
    slot_count = left.shape[1]
    block_size = left.shape[2]

    def one_row(row_data):
        own_blocks, own_pattern, own_local = row_data
        used_local = lax.dynamic_slice_in_dim(own_local, first_slot, slot_span, 0)
        used_blocks = lax.dynamic_slice_in_dim(own_blocks, first_slot, slot_span, 0)
        fetched = jnp.take(near_blocks, used_local, axis=0).reshape(
            slot_span, slot_count, block_size * block_size
        )
        fetched_pattern = jnp.take(near_pattern, used_local, axis=0)
        select = (fetched_pattern[:, None, :] == own_pattern[None, :, None]).astype(jnp.bfloat16)
        aligned = jnp.einsum("kjl,klx->kjx", select, fetched, preferred_element_type=jnp.bfloat16)
        aligned = aligned.reshape(slot_span, slot_count, block_size, block_size)
        return jnp.einsum("kab,kjbc->jac", used_blocks, aligned, preferred_element_type=jnp.float32)

    return lax.map(one_row, (left, left_pattern, local_index))


def regroup(updated, targets):
    device_count = lax.axis_size(("row", "col"))
    row_count = updated.shape[0]
    half_slots = updated.shape[1]
    block_size = updated.shape[2]
    item_count = row_count * half_slots
    capacity = max(2, 3 * item_count // device_count + 1)
    flat_targets = targets.reshape(item_count)
    same_owner = flat_targets[:, None] == flat_targets[None, :]
    earlier = jnp.arange(item_count)[:, None] > jnp.arange(item_count)[None, :]
    rank_index = jnp.sum((same_owner & earlier).astype(jnp.int32), axis=1)
    destination = flat_targets * capacity + rank_index
    select = (
        jnp.arange(device_count * capacity, dtype=jnp.int32)[:, None] == destination[None, :]
    ).astype(jnp.bfloat16)
    outgoing = jnp.dot(
        select,
        updated.reshape(item_count, block_size * block_size),
        preferred_element_type=jnp.float32,
    ).astype(jnp.bfloat16)
    outgoing = outgoing.reshape(device_count, capacity, block_size, block_size)
    received = lax.all_to_all(outgoing, ("row", "col"), split_axis=0, concat_axis=0, tiled=True)
    return received.reshape(1, 1, device_count, capacity, block_size, block_size)


def shards(blocks, pattern, owner_map):
    row_count = blocks.shape[0]
    slot_count = blocks.shape[1]
    block_size = blocks.shape[2]
    half_slots = slot_count // 2
    device_count = lax.axis_size(("row", "col"))
    total_rows = device_count * row_count
    position = lax.axis_index(("row", "col"))
    layer_index = lax.axis_index("depth")
    inv_scale = 1.0 / math.sqrt(block_size * slot_count)
    targets = owner_map[0, :, :, 0]
    offsets = list(range(HOPS, 0, -1)) + list(range(-1, -HOPS - 1, -1))
    arrivals = [passed_along((blocks, pattern), ("row", "col"), offset) for offset in offsets]
    near_blocks = jnp.concatenate(
        [arrived[0] for arrived in arrivals[:HOPS]]
        + [blocks]
        + [arrived[0] for arrived in arrivals[HOPS:]],
        axis=0,
    )
    near_pattern = jnp.concatenate(
        [arrived[1] for arrived in arrivals[:HOPS]]
        + [pattern]
        + [arrived[1] for arrived in arrivals[HOPS:]],
        axis=0,
    )
    first_row = (position - HOPS) * row_count
    local_index = (pattern - first_row) % total_rows
    first_slot = layer_index * half_slots
    partial_value = product_rows(
        blocks, pattern, local_index, near_blocks, near_pattern, first_slot, half_slots
    )
    squared = (lax.psum(partial_value, "depth") * inv_scale).astype(jnp.bfloat16)
    w_arrivals = [passed_along(squared, ("row", "col"), offset) for offset in offsets]
    near_squared = jnp.concatenate(w_arrivals[:HOPS] + [squared] + w_arrivals[HOPS:], axis=0)
    partial_value = product_rows(
        blocks, pattern, local_index, near_squared, near_pattern, first_slot, half_slots
    )
    cubic_term = lax.psum_scatter(
        partial_value.astype(jnp.bfloat16), "depth", scatter_dimension=1, tiled=True
    ).astype(jnp.float32)
    own_blocks = lax.dynamic_slice_in_dim(blocks, first_slot, half_slots, 1)
    updated = (1.5 * own_blocks.astype(jnp.float32) - 0.5 * inv_scale * cubic_term).astype(
        jnp.bfloat16
    )
    return regroup(updated, targets)


def solution(mesh):
    placed = (
        P(("groups", "row", "col"), None, None, None),
        P(("groups", "row", "col"), None),
        P("depth", ("groups", "row", "col"), None, None),
    )
    return jax.shard_map(
        shards,
        mesh=mesh,
        in_specs=placed,
        out_specs=P("depth", ("groups", "row", "col"), None, None, None, None),
        check_vma=False,
    )
```

profile of v0, /device:TPU:0, one launch (start us, length us, event | category | flops | bytes accessed | tf_op | source)
XLA Modules:
  0.0 730.0 jit_solution(2106381814681235641)
XLA Ops:
  6.5 4.0 collective-permute-start.6
  16.3 108.6 %collective-permute-done = s32[4,20]{1,0:T(4,128)S(1)} collective-permute-done((s32[4,20]{1,0:T(4,128)}, s32[4,20]{1,0:T(4,128)S(1)}, u32[]{:S(2)}, u32[]{:S(2)}) %collective-permute-start) | collective-permute-done | bytes 352 | tf_op jit(solution)/shard_map/ppermute | solution.py:13
  125.0 4.7 collective-permute-start.3
  137.0 27.6 %collective-permute-done.5 = s32[4,20]{1,0:T(4,128)S(1)} collective-permute-done((s32[4,20]{1,0:T(4,128)}, s32[4,20]{1,0:T(4,128)S(1)}, u32[]{:S(2)}, u32[]{:S(2)}) %collective-permute-start.5) | collective-permute-done | bytes 352 | tf_op jit(solution)/shard_map/ppermute | solution.py:13
  165.5 4.1 collective-permute-start.11
  174.1 20.3 %collective-permute-done.10 = bf16[4,20,64,64]{3,2,1,0:T(8,128)(2,1)} collective-permute-done((bf16[4,20,64,64]{3,2,1,0:T(8,128)(2,1)}, bf16[4,20,64,64]{3,2,1,0:T(8,128)(2,1)}, u32[]{:S(2)}, u32[]{:S(2)}) %collective-permute-start.10) | collective-permute-done | bytes 655392 | tf_op jit(solution)/shard_map/ppermute | solution.py:13
  195.8 23.1 %collective-permute-done.11 = bf16[4,20,64,64]{3,2,1,0:T(8,128)(2,1)S(1)} collective-permute-done((bf16[4,20,64,64]{3,2,1,0:T(8,128)(2,1)}, bf16[4,20,64,64]{3,2,1,0:T(8,128)(2,1)S(1)}, u32[]{:S(2)}, u32[]{:S(2)}) %collective-permute-start.11) | collective-permute-done | bytes 655392 | tf_op jit(solution)/shard_map/ppermute | solution.py:13
  222.7 107.9 %while.26 = (s32[]{:T(128)}, f32[4,20,64,64]{3,2,1,0:T(8,128)}, s32[4,20]{1,0:T(4,128)S(1)}, s32[]{:T(128)}, s32[28,20]{1,0:T(8,128)S(1)}, /*index=5*/s32[4,20]{...) while((s32[]{:T(128)}, f32[4,20,64,64]{3,2,1,0:T(8,128)}, ...), condition=%wide.region_2.5_spmd, body=%wide.region_1.4_spmd.sunk | while | flops 138450080 | bytes 20162052 | solution.py:33
  222.8 6.5 gather_fusion
  231.6 3.9 reshape.164
  239.7 5.0 reshape.165
  249.8 6.5 gather_fusion
  258.6 3.9 reshape.164
  266.7 5.0 reshape.165
  276.8 6.5 gather_fusion
  293.7 5.0 reshape.165
  303.8 6.5 gather_fusion
  320.6 5.0 reshape.165
  330.7 51.8 %all-reduce.4.cloned.1.call-done = f32[4,20,64,64]{3,2,1,0:T(8,128)} async-done(((f32[4,20,64,64]{3,2,1,0:T(8,128)}), f32[4,20,64,64]{3,2,1,0:T(8,128)}) %all-reduce.4.cloned.1.call-update) | async-done | bytes 1310736 | tf_op jit(solution)/shard_map/psum | solution.py:92
  395.1 108.6 %collective-permute-done.12 = bf16[4,20,64,64]{3,2,1,0:T(8,128)(2,1)} collective-permute-done((bf16[4,20,64,64]{3,2,1,0:T(8,128)(2,1)}, bf16[4,20,64,64]{3,2,1,0:T(8,128)(2,1)}, u32[]{:S(2)}, u32[]{:S(2)}) %collective-permute-start.12) | collective-permute-done | bytes 655392 | tf_op jit(solution)/shard_map/ppermute | solution.py:13
  507.7 26.7 %collective-permute-done.17 = bf16[4,20,64,64]{3,2,1,0:T(8,128)(2,1)S(1)} collective-permute-done((bf16[4,20,64,64]{3,2,1,0:T(8,128)(2,1)}, bf16[4,20,64,64]{3,2,1,0:T(8,128)(2,1)S(1)}, u32[]{:S(2)}, u32[]{:S(2)}) %collective-permute-start.17) | collective-permute-done | bytes 655392 | tf_op jit(solution)/shard_map/ppermute | solution.py:13
  538.1 98.6 %while.27 = (s32[]{:T(128)}, bf16[4,20,64,64]{2,3,1,0:T(8,128)(2,1)}, s32[4,20]{1,0:T(4,128)S(1)}, s32[]{:T(128)}, s32[28,20]{1,0:T(8,128)S(1)}, /*index=5*/s32[...) while((s32[]{:T(128)}, ...), condition=%wide.region_5.8_spmd, body=%wide.region_4.7_spmd.sunk | while | flops 138450080 | bytes 18851332 | solution.py:33
  538.2 6.5 gather_fusion.2
  555.1 5.0 reshape.171
  562.9 6.5 gather_fusion.2
  579.8 5.0 reshape.171
  587.6 6.5 gather_fusion.2
  604.4 5.0 reshape.171
  612.2 6.5 gather_fusion.2
  629.1 5.0 reshape.171
  641.0 41.1 %all-reduce.6.cloned.1.call-done = bf16[4,20,64,64]{2,3,1,0:T(8,128)(2,1)} async-done(((bf16[4,20,64,64]{2,3,1,0:T(8,128)(2,1)}), bf16[4,20,64,64]{2,3,1,0:T(8,128)(2,1)}) %all-reduce.6.cloned.1.call-update) | async-done | bytes 655376
  688.7 31.8 %all_to_all.5 = bf16[8,2,32768]{2,1,0:T(2,128)(2,1)S(1)} all-to-all(bf16[8,2,32768]{2,1,0:T(2,128)(2,1)S(1)} %reshape.146), channel_id=1, replica_groups=mesh['groups'=2,'row'=4,'col'=2,'depth'=2] {'row','col'}, dimensions={0} | all-to-all | bytes 2097152 | tf_op jit(solution)/shard_map/all_to_all | solution.py:57
  (157 shorter events, 163.7 us)
Async XLA Ops:
  6.5 375.9 %all-reduce.4.cloned.1.call-start = ((), (), s32[]{:S(2)}) async-start(), calls=%async_computation.1 | async-start | bytes 5242880 | tf_op jit(solution)/shard_map/psum | solution.py:92
  6.5 159.0 %collective-permute-start.6 = (bf16[4,20,64,64]{3,2,1,0:T(8,128)(2,1)}, bf16[4,20,64,64]{3,2,1,0:T(8,128)(2,1)}, u32[]{:S(2)}, u32[]{:S(2)}) collective-permute-start(bf16[4,20,64,64]{3,2,1,0:T(8,128)(2,1)} %param.11), channel_id=1, source_target_pairs={{0,6},{2,8},{4,10},{6,12},{8,14},{10,0},{12,2},{14,4},{1,7},{3,9},... | collective-permute-start | bytes 1966088 | tf_op jit(solution)/shard_map/ppermute | solution.py:13
  10.5 160.5 %collective-permute-start.7 = (bf16[4,20,64,64]{3,2,1,0:T(8,128)(2,1)}, bf16[4,20,64,64]{3,2,1,0:T(8,128)(2,1)S(1)}, u32[]{:S(2)}, u32[]{:S(2)}) collective-permute-start(bf16[4,20,64,64]{3,2,1,0:T(8,128)(2,1)} %param.11), channel_id=1, source_target_pairs={{0,4},{2,6},{4,8},{6,10},{8,12},{10,14},{12,0},{14,2},{1,5},{3,7},... | collective-permute-start | bytes 1966088 | tf_op jit(solution)/shard_map/ppermute | solution.py:13
  12.1 159.2 %collective-permute-start.8 = (bf16[4,20,64,64]{3,2,1,0:T(8,128)(2,1)}, bf16[4,20,64,64]{3,2,1,0:T(8,128)(2,1)S(1)}, u32[]{:S(2)}, u32[]{:S(2)}) collective-permute-start(bf16[4,20,64,64]{3,2,1,0:T(8,128)(2,1)} %param.11), channel_id=1, source_target_pairs={{0,2},{2,4},{4,6},{6,8},{8,10},{10,12},{12,14},{14,0},{1,3},{3,5},... | collective-permute-start | bytes 1966088 | tf_op jit(solution)/shard_map/ppermute | solution.py:13
  13.6 111.4 %collective-permute-start = (s32[4,20]{1,0:T(4,128)}, s32[4,20]{1,0:T(4,128)S(1)}, u32[]{:S(2)}, u32[]{:S(2)}) collective-permute-start(s32[4,20]{1,0:T(4,128)} %param.12), channel_id=1, source_target_pairs={{0,6},{2,8},{4,10},{6,12},{8,14},{10,0},{12,2},{14,4},{1,7},{3,9},... | collective-permute-start | bytes 968 | tf_op jit(solution)/shard_map/ppermute | solution.py:13
  14.8 110.2 %collective-permute-start.1 = (s32[4,20]{1,0:T(4,128)}, s32[4,20]{1,0:T(4,128)S(1)}, u32[]{:S(2)}, u32[]{:S(2)}) collective-permute-start(s32[4,20]{1,0:T(4,128)} %param.12), channel_id=1, source_target_pairs={{0,4},{2,6},{4,8},{6,10},{8,12},{10,14},{12,0},{14,2},{1,5},{3,7},... | collective-permute-start | bytes 968 | tf_op jit(solution)/shard_map/ppermute | solution.py:13
  125.0 6.5 collective-permute-start.2
  125.0 8.1 %collective-permute-start.3 = (s32[4,20]{1,0:T(4,128)}, s32[4,20]{1,0:T(4,128)S(1)}, u32[]{:S(2)}, u32[]{:S(2)}) collective-permute-start(s32[4,20]{1,0:T(4,128)} %param.12), channel_id=1, source_target_pairs={{0,14},{2,0},{4,2},{6,4},{8,6},{10,8},{12,10},{14,12},{1,15},{3,1}... | collective-permute-start | bytes 968 | tf_op jit(solution)/shard_map/ppermute | solution.py:13
  131.5 5.4 collective-permute-start.4
  133.1 39.4 %collective-permute-start.9 = (bf16[4,20,64,64]{3,2,1,0:T(8,128)(2,1)}, bf16[4,20,64,64]{3,2,1,0:T(8,128)(2,1)}, u32[]{:S(2)}, u32[]{:S(2)}) collective-permute-start(bf16[4,20,64,64]{3,2,1,0:T(8,128)(2,1)} %param.11), channel_id=1, source_target_pairs={{0,14},{2,0},{4,2},{6,4},{8,6},{10,8},{12,10},{14,12},{1,15},{3,1}... | collective-permute-start | bytes 1966088 | tf_op jit(solution)/shard_map/ppermute | solution.py:13
  136.9 27.7 %collective-permute-start.5 = (s32[4,20]{1,0:T(4,128)}, s32[4,20]{1,0:T(4,128)S(1)}, u32[]{:S(2)}, u32[]{:S(2)}) collective-permute-start(s32[4,20]{1,0:T(4,128)} %param.12), channel_id=1, source_target_pairs={{0,10},{2,12},{4,14},{6,0},{8,2},{10,4},{12,6},{14,8},{1,11},{3,13... | collective-permute-start | bytes 968 | tf_op jit(solution)/shard_map/ppermute | solution.py:13
  164.6 29.8 %collective-permute-start.10 = (bf16[4,20,64,64]{3,2,1,0:T(8,128)(2,1)}, bf16[4,20,64,64]{3,2,1,0:T(8,128)(2,1)}, u32[]{:S(2)}, u32[]{:S(2)}) collective-permute-start(bf16[4,20,64,64]{3,2,1,0:T(8,128)(2,1)} %param.11), channel_id=1, source_target_pairs={{0,12},{2,14},{4,0},{6,2},{8,4},{10,6},{12,8},{14,10},{1,13},{3,15... | collective-permute-start | bytes 1966088 | tf_op jit(solution)/shard_map/ppermute | solution.py:13
  165.5 53.5 %collective-permute-start.11 = (bf16[4,20,64,64]{3,2,1,0:T(8,128)(2,1)}, bf16[4,20,64,64]{3,2,1,0:T(8,128)(2,1)S(1)}, u32[]{:S(2)}, u32[]{:S(2)}) collective-permute-start(bf16[4,20,64,64]{3,2,1,0:T(8,128)(2,1)} %param.11), channel_id=1, source_target_pairs={{0,10},{2,12},{4,14},{6,0},{8,2},{10,4},{12,6},{14,8},{1,11},{3,13... | collective-permute-start | bytes 1966088 | tf_op jit(solution)/shard_map/ppermute | solution.py:13
  171.0 1.3 copy-start.3
  174.0 48.7 %copy-start.4 = (s32[4,20]{1,0:T(4,128)S(1)}, s32[4,20]{1,0:T(4,128)}, u32[]{:S(2)}) copy-start(s32[4,20]{1,0:T(4,128)} %param.12) | copy-start | bytes 964
  219.2 3.5 copy-start
  330.7 351.4 %all-reduce.6.cloned.1.call-start = ((), (), s32[]{:S(2)}) async-start(), calls=%async_computation.2 | async-start | bytes 2621440
  385.7 118.0 %collective-permute-start.12 = (bf16[4,20,64,64]{3,2,1,0:T(8,128)(2,1)}, bf16[4,20,64,64]{3,2,1,0:T(8,128)(2,1)}, u32[]{:S(2)}, u32[]{:S(2)}) collective-permute-start(bf16[4,20,64,64]{3,2,1,0:T(8,128)(2,1)} %multiply_convert_fusion), channel_id=1, source_target_pairs={{0,6},{2,8},{4,10},{6,12},{8,14},{10,0},{12,2},{14,4},{1,7},{3,9},... | collective-permute-start | bytes 1966088 | tf_op jit(solution)/shard_map/ppermute | solution.py:13
  388.3 116.8 %collective-permute-start.13 = (bf16[4,20,64,64]{3,2,1,0:T(8,128)(2,1)}, bf16[4,20,64,64]{3,2,1,0:T(8,128)(2,1)S(1)}, u32[]{:S(2)}, u32[]{:S(2)}) collective-permute-start(bf16[4,20,64,64]{3,2,1,0:T(8,128)(2,1)} %multiply_convert_fusion), channel_id=1, source_target_pairs={{0,4},{2,6},{4,8},{6,10},{8,12},{10,14},{12,0},{14,2},{1,5},{3,7},... | collective-permute-start | bytes 1966088 | tf_op jit(solution)/shard_map/ppermute | solution.py:13
  389.8 115.5 %collective-permute-start.14 = (bf16[4,20,64,64]{3,2,1,0:T(8,128)(2,1)}, bf16[4,20,64,64]{3,2,1,0:T(8,128)(2,1)S(1)}, u32[]{:S(2)}, u32[]{:S(2)}) collective-permute-start(bf16[4,20,64,64]{3,2,1,0:T(8,128)(2,1)} %multiply_convert_fusion), channel_id=1, source_target_pairs={{0,2},{2,4},{4,6},{6,8},{8,10},{10,12},{12,14},{14,0},{1,3},{3,5},... | collective-permute-start | bytes 1966088 | tf_op jit(solution)/shard_map/ppermute | solution.py:13
  391.3 116.0 %collective-permute-start.15 = (bf16[4,20,64,64]{3,2,1,0:T(8,128)(2,1)}, bf16[4,20,64,64]{3,2,1,0:T(8,128)(2,1)S(1)}, u32[]{:S(2)}, u32[]{:S(2)}) collective-permute-start(bf16[4,20,64,64]{3,2,1,0:T(8,128)(2,1)} %multiply_convert_fusion), channel_id=1, source_target_pairs={{0,14},{2,0},{4,2},{6,4},{8,6},{10,8},{12,10},{14,12},{1,15},{3,1}... | collective-permute-start | bytes 1966088 | tf_op jit(solution)/shard_map/ppermute | solution.py:13
  394.5 113.0 %collective-permute-start.16 = (bf16[4,20,64,64]{3,2,1,0:T(8,128)(2,1)}, bf16[4,20,64,64]{3,2,1,0:T(8,128)(2,1)S(1)}, u32[]{:S(2)}, u32[]{:S(2)}) collective-permute-start(bf16[4,20,64,64]{3,2,1,0:T(8,128)(2,1)} %multiply_convert_fusion), channel_id=1, source_target_pairs={{0,12},{2,14},{4,0},{6,2},{8,4},{10,6},{12,8},{14,10},{1,13},{3,15... | collective-permute-start | bytes 1966088 | tf_op jit(solution)/shard_map/ppermute | solution.py:13
  503.7 30.7 %collective-permute-start.17 = (bf16[4,20,64,64]{3,2,1,0:T(8,128)(2,1)}, bf16[4,20,64,64]{3,2,1,0:T(8,128)(2,1)S(1)}, u32[]{:S(2)}, u32[]{:S(2)}) collective-permute-start(bf16[4,20,64,64]{3,2,1,0:T(8,128)(2,1)} %multiply_convert_fusion), channel_id=1, source_target_pairs={{0,10},{2,12},{4,14},{6,0},{8,2},{10,4},{12,6},{14,8},{1,11},{3,13... | collective-permute-start | bytes 1966088 | tf_op jit(solution)/shard_map/ppermute | solution.py:13
  505.1 1.7 copy-start.2
  534.6 3.5 copy-start.1
  636.8 2.0 copy-start.5
  636.8 2.8 copy-start.6
Sparse Core Ops, SparseCore 0:
  330.8 51.6 all-reduce.3
  636.9 45.1 all-reduce.5
where the time goes:
time: 732 us; the launch traced here: 730 us
  waiting for transfers between devices  410 us (56%)
  local copies, waits for them, and re-layouts  164 us (22%)
  matrix products  50.8 us (7%)
  starting transfers between devices  33 us (5%)
  blocking collectives  31.8 us (4%)
  other arithmetic  26.2 us (4%)
  between operations  14.3 us (2%)
    ppermute x18, waiting for transfers between devices, passed_along(): lax.ppermute(value, axis, [(i, (i + by) % peers) for i in range(peers)])  317 us
    psum x1, waiting for transfers between devices, shards(): lax.psum(partial_value, 'depth') * inv_scale  51.8 us
    gather x8, local copies, waits for them, and re-layouts, one_row(): jnp.take(near_blocks, used_local, axis=0)  51.6 us
    unnamed x3, waiting for transfers between devices  41.2 us
    reshape x8, local copies, waits for them, and re-layouts, one_row(): aligned = aligned.reshape(slot_span, slot_count, block_size, block_size)  39.8 us
    ppermute x18, starting transfers between devices, passed_along(): lax.ppermute(value, axis, [(i, (i + by) % peers) for i in range(peers)])  33 us
    all_to_all x1, blocking collectives, regroup(): lax.all_to_all(outgoing, ('row', 'col'), split_axis=0, concat_axis=0, til...  31.8 us
    reshape x8, local copies, waits for them, and re-layouts, one_row(): jnp.take(near_blocks, used_local, axis=0)  31.5 us
  transfers between devices with their start and end apart: 20, of which 9 were waited for; matrix products, arithmetic and copies ran while one was open for 2% of the time, Pallas kernels for 0%

commit v1 on v0

--- a/solution.py
+++ b/solution.py
@@ -1,11 +1,15 @@
+import functools
 import math
 
 import jax
 import jax.numpy as jnp
 from jax import lax
+from jax.experimental import pallas as pl
+from jax.experimental.pallas import tpu as pltpu
 from jax.sharding import PartitionSpec as P
 
 HOPS = 3
+MESH = pl.DeviceIdType.MESH
 
 
 def passed_along(value, axis, by):
@@ -105,14 +109,255 @@
     return regroup(updated, targets)
 
 
+def gather_kernel(
+    dims, blocks_ref, meta_ref, packed, meta_v,
+    send_sem, recv_sem, sib_sem, meta_send, meta_recv,
+):
+    n_row, n_col, rows, slots, size, capacity = dims
+    devices = n_row * n_col
+    part = rows * size
+    half_rows = slots // 2 * size
+    z, x, h = lax.axis_index("row"), lax.axis_index("col"), lax.axis_index("depth")
+    me = z * n_col + x
+    across = n_col - 1 - x
+
+    def device(to_z, to_x, to_h):
+        return {"row": to_z, "col": to_x, "depth": to_h}
+
+    sibling = device(z, x, 1 - h)
+
+    barrier = pltpu.get_barrier_semaphore()
+    for step in range(1, devices):
+        peer = lax.rem(me + step, devices)
+        pl.semaphore_signal(
+            barrier, inc=1, device_id=device(peer // n_col, lax.rem(peer, n_col), h),
+            device_id_type=MESH,
+        )
+    pl.semaphore_signal(barrier, inc=1, device_id=sibling, device_id_type=MESH)
+
+    for pair in range(rows // 2):
+        packed[me, : slots * size, pair * 2 * size : (pair + 1) * 2 * size] = jnp.concatenate(
+            [blocks_ref[2 * pair + t].reshape(slots * size, size) for t in range(2)], axis=1
+        )
+    for source in range(devices):
+        packed[source, slots * size :, :] = jnp.zeros((size, part), jnp.bfloat16)
+    meta_v[me] = meta_ref[...]
+    pl.semaphore_wait(barrier, devices)
+
+    def meta_copy(step):
+        peer = lax.rem(me + step, devices)
+        return pltpu.make_async_remote_copy(
+            src_ref=meta_v.at[me], dst_ref=meta_v.at[me],
+            send_sem=meta_send.at[step], recv_sem=meta_recv.at[step],
+            device_id=device(peer // n_col, lax.rem(peer, n_col), h), device_id_type=MESH,
+        )
+
+    def piece(position, which):
+        return packed.at[position, pl.ds(which * half_rows, half_rows), :]
+
+    def copy(position, k, target, landed, which=None):
+        ref = piece(position, h if which is None else which)
+        return pltpu.make_async_remote_copy(
+            src_ref=ref, dst_ref=ref, send_sem=send_sem.at[position, k],
+            recv_sem=landed.at[position], device_id=target, device_id_type=MESH,
+        )
+
+    sends = []
+
+    def start(valid, position, k, target, landed):
+        @pl.when(valid)
+        def _():
+            copy(position, k, target, landed).start()
+        sends.append((valid, position, k, target, landed))
+
+    for step in range(1, devices):
+        meta_copy(step).start()
+    start(z > 0, me, 0, device(z - 1, x, h), recv_sem)
+    start(z < n_row - 1, me, 1, device(z + 1, x, h), recv_sem)
+    start(z >= 0, me, 2, device(z, across, h), recv_sem)
+
+    def from_z(distance, way):
+        source = z + way * distance
+        valid = (source >= 0) & (source < n_row)
+        position = source * n_col + x
+
+        @pl.when(valid)
+        def _():
+            copy(position, 0, sibling, recv_sem).wait_recv()
+        start(valid & (z - way >= 0) & (z - way < n_row), position, 0, device(z - way, x, h), recv_sem)
+        start(valid, position, 1, device(z, across, h), recv_sem)
+        start(valid, position, 2, sibling, sib_sem)
+
+    def from_x(distance, way):
+        source = z + way * distance
+        valid = (source >= 0) & (source < n_row)
+        position = source * n_col + across
+
+        @pl.when(valid)
+        def _():
+            copy(position, 0, sibling, recv_sem).wait_recv()
+        start(valid, position, 0, sibling, sib_sem)
+
+    for distance in range(1, n_row):
+        from_z(distance, 1)
+        from_z(distance, -1)
+        if distance == 1:
+            from_x(0, 1)
+        else:
+            from_x(distance - 1, 1)
+            from_x(distance - 1, -1)
+    from_x(n_row - 1, 1)
+    from_x(n_row - 1, -1)
+
+    for step in range(1, devices):
+        meta_copy(step).wait()
+    for step in range(1, devices):
+        position = lax.rem(me + step, devices)
+        copy(position, 0, sibling, sib_sem, 1 - h).wait_recv()
+    for valid, position, k, target, landed in sends:
+        @pl.when(valid)
+        def _(position=position, k=k, target=target, landed=landed):
+            copy(position, k, target, landed).wait_send()
+
+
+def dense_kernel(dims, packed, meta_s, out_ref, x_ref, sq_ref, mask_ref, up_ref):
+    n_row, n_col, rows, slots, size, capacity = dims
+    devices = n_row * n_col
+    total = devices * rows
+    width = total * size
+    part = rows * size
+    me = lax.axis_index("row") * n_col + lax.axis_index("col")
+
+    lane = lax.broadcasted_iota(jnp.int32, (1, 2 * size), 1)
+
+    def expand(source, carry):
+        for row in range(rows):
+            lanes = row // 2 * 2 * size
+            at = row % 2 * size
+            for pair in range(total // 2):
+                slot = [meta_s[source, 0, row * total + 2 * pair + t] for t in range(2)]
+                both = [
+                    packed[source, pl.ds(pl.multiple_of(slot[t] * size, size), size), lanes : lanes + 2 * size]
+                    for t in range(2)
+                ]
+                spot = slice(pair * 2 * size, (pair + 1) * 2 * size)
+                x_ref[pl.ds(pl.multiple_of(source * part + row * size, size), size), spot] = (
+                    jnp.concatenate([both[t][:, at : at + size] for t in range(2)], axis=1)
+                )
+                kept = [(slot[t] < slots).astype(jnp.float32) for t in range(2)]
+                mask_ref[source, row : row + 1, spot] = jnp.where(lane < size, kept[0], kept[1])
+        return carry
+
+    lax.fori_loop(0, devices, expand, 0)
+
+    inv_scale = 1.0 / math.sqrt(size * slots)
+    tile = 4 * 2 * size
+
+    def square(source, carry):
+        own = pl.ds(pl.multiple_of(source * part, part), part)
+        for column in range(width // tile):
+            spot = slice(column * tile, (column + 1) * tile)
+            value = jnp.dot(x_ref[own, :], x_ref[:, spot], preferred_element_type=jnp.float32)
+            kept = jnp.broadcast_to(mask_ref[source, :, spot][:, None, :], (rows, size, tile))
+            sq_ref[own, spot] = (value * inv_scale * kept.reshape(part, tile)).astype(jnp.bfloat16)
+        return carry
+
+    lax.fori_loop(0, devices, square, 0)
+
+    def cube(source, carry):
+        own = pl.ds(pl.multiple_of(source * part, part), part)
+        for column in range(width // tile):
+            spot = slice(column * tile, (column + 1) * tile)
+            value = jnp.dot(x_ref[own, :], sq_ref[:, spot], preferred_element_type=jnp.float32)
+            value = 1.5 * x_ref[own, spot].astype(jnp.float32) - (0.5 * inv_scale) * value
+            value = value.astype(jnp.bfloat16)
+            for t in range(4):
+                up_ref[column * 4 + t] = value[:, t * 2 * size : (t + 1) * 2 * size]
+        for rank in range(capacity):
+            code = meta_s[source, 1, me * capacity + rank]
+            found = jnp.maximum(code, 0)
+            column = found & (total - 1)
+            row = found >> (total.bit_length() - 1)
+            block = up_ref[column >> 1, pl.ds(pl.multiple_of(row * size, size), size), :]
+            block = block.astype(jnp.float32)
+            block = jnp.where((column & 1) == 0, block[:, :size], block[:, size:])
+            out_ref[source, rank] = jnp.where(code >= 0, block, 0.0).astype(jnp.bfloat16)
+        return carry
+
+    lax.fori_loop(0, devices, cube, 0)
+
+
+def dense_shards(blocks, pattern, owner_map):
+    rows, slots, size, _ = blocks.shape
+    n_row, n_col = lax.axis_size("row"), lax.axis_size("col")
+    devices = n_row * n_col
+    total = devices * rows
+    items = rows * (slots // 2)
+    capacity = max(2, 3 * items // devices + 1)
+    h = lax.axis_index("depth")
+
+    slot_number = jnp.arange(slots, dtype=jnp.int32)[None, :, None]
+    named = pattern[:, :, None] == jnp.arange(total, dtype=jnp.int32)[None, None, :]
+    slot_of = slots + jnp.sum(jnp.where(named, slot_number - slots, 0), axis=1)
+
+    targets = owner_map.reshape(items)
+    earlier = jnp.arange(items)[:, None] > jnp.arange(items)[None, :]
+    rank = jnp.sum(((targets[:, None] == targets[None, :]) & earlier).astype(jnp.int32), axis=1)
+    columns = lax.dynamic_slice_in_dim(pattern, h * (slots // 2), slots // 2, 1)
+    code = jnp.arange(rows, dtype=jnp.int32)[:, None] * total + columns
+    placed = jnp.arange(devices * capacity, dtype=jnp.int32)[:, None] == (targets * capacity + rank)[None, :]
+    item_at = jnp.sum(jnp.where(placed, code.reshape(1, items) + 1, 0), axis=1) - 1
+    lanes = 128
+    meta = jnp.concatenate(
+        [slot_of.reshape(1, lanes), item_at.reshape(1, lanes), jnp.zeros((6, lanes), jnp.int32)], axis=0
+    )
+    dims = (n_row, n_col, rows, slots, size, capacity)
+    width = total * size
+    vmem = pl.BlockSpec(memory_space=pltpu.VMEM)
+    gathered, gathered_meta = pl.pallas_call(
+        functools.partial(gather_kernel, dims),
+        out_shape=(
+            jax.ShapeDtypeStruct((devices, (slots + 1) * size, rows * size), jnp.bfloat16),
+            jax.ShapeDtypeStruct((devices, 8, lanes), jnp.int32),
+        ),
+        in_specs=[vmem, vmem],
+        out_specs=(vmem, vmem),
+        scratch_shapes=[
+            pltpu.SemaphoreType.DMA((devices, 3)),
+            pltpu.SemaphoreType.DMA((devices,)),
+            pltpu.SemaphoreType.DMA((devices,)),
+            pltpu.SemaphoreType.DMA((devices,)),
+            pltpu.SemaphoreType.DMA((devices,)),
+        ],
+        compiler_params=pltpu.CompilerParams(
+            collective_id=0, has_side_effects=True, vmem_limit_bytes=24 * 1024 * 1024
+        ),
+    )(blocks, meta)
+    out = pl.pallas_call(
+        functools.partial(dense_kernel, dims),
+        out_shape=jax.ShapeDtypeStruct((devices, capacity, size, size), jnp.bfloat16),
+        in_specs=[vmem, pl.BlockSpec(memory_space=pltpu.SMEM)],
+        out_specs=vmem,
+        scratch_shapes=[
+            pltpu.VMEM((width, width), jnp.bfloat16),
+            pltpu.VMEM((width, width), jnp.bfloat16),
+            pltpu.VMEM((devices, rows, width), jnp.float32),
+            pltpu.VMEM((total // 2, rows * size, 2 * size), jnp.bfloat16),
+        ],
+        compiler_params=pltpu.CompilerParams(vmem_limit_bytes=40 * 1024 * 1024),
+    )(gathered, gathered_meta)
+    return out.reshape(1, 1, devices, capacity, size, size)
+
+
 def solution(mesh):
     placed = (
         P(("groups", "row", "col"), None, None, None),
         P(("groups", "row", "col"), None),
         P("depth", ("groups", "row", "col"), None, None),
     )
+    small = mesh.shape["row"] * mesh.shape["col"] <= 8 and mesh.shape["col"] == 2
     return jax.shard_map(
-        shards,
+        dense_shards if small else shards,
         mesh=mesh,
         in_specs=placed,
         out_specs=P("depth", ("groups", "row", "col"), None, None, None, None),

time: 732 us -> 89.2 us (0.12)
  waiting for transfers between devices: 410 us -> 0 us
  local copies, waits for them, and re-layouts: 164 us -> 2.94 us
  Pallas kernels: 0 us -> 83.4 us
  matrix products: 50.8 us -> 0 us
  starting transfers between devices: 33 us -> 0 us
  blocking collectives: 31.8 us -> 0 us
  other arithmetic: 26.2 us -> 2.58 us
  between operations: 14.3 us -> 0.04 us
    ppermute x18 -> x0, waiting for transfers between devices: 317 us -> none  [passed_along(): lax.ppermute(value, axis, [(i, (i + by) % peers) for i in range(peers)])]
    pallas_call x0 -> x2, Pallas kernels: none -> 83.4 us  [the longest x1 45 us: dense_shards(): pl.pallas_call(functools.partial(dense_kernel, dims), out_shape=jax.Shape...]
    reshape x18 -> x1, local copies, waits for them, and re-layouts: 74.1 us -> 0.09 us  [dense_shards(): targets = owner_map.reshape(items)]
    gather x16 -> x0, local copies, waits for them, and re-layouts: 56 us -> none  [the longest x8 51.6 us: one_row(): jnp.take(near_blocks, used_local, axis=0)]
    psum x1 -> x0, waiting for transfers between devices: 51.8 us -> none  [shards(): lax.psum(partial_value, 'depth') * inv_scale]
    dot_general x17 -> x0, matrix products: 50.8 us -> none  [the longest x8 28.3 us: one_row(): jnp.einsum('kjl,klx->kjx', select, fetched, preferred_element_type=jnp.bf...]
    unnamed x3 -> x0, waiting for transfers between devices: 41.2 us -> none
    ppermute x18 -> x0, starting transfers between devices: 33 us -> none  [passed_along(): lax.ppermute(value, axis, [(i, (i + by) % peers) for i in range(peers)])]
  transfers between devices with their start and end apart: 20 -> 0, of which waited for: 9 -> 0; matrix products, arithmetic and copies ran while one was open for 2% -> 0% of each run, Pallas kernels for 0% -> 0%
where the time goes in v1:
time: 89.2 us; the launch traced here: 89 us
  Pallas kernels  83.4 us (93%)
  local copies, waits for them, and re-layouts  2.94 us (3%)
  other arithmetic  2.58 us (3%)
    pallas_call x1, Pallas kernels, dense_shards(): pl.pallas_call(functools.partial(dense_kernel, dims), out_shape=jax.Shape...  45 us
    pallas_call x1, Pallas kernels, dense_shards(): pl.pallas_call(functools.partial(gather_kernel, dims), out_shape=(jax.Sha...  38.4 us
    unnamed x4, local copies, waits for them, and re-layouts  2.61 us

profile of v1, /device:TPU:0, one launch (start us, length us, event | category | flops | bytes accessed | tf_op | source)
XLA Modules:
  0.0 89.0 jit_solution(6618776794014873723)
XLA Ops:
  0.0 0.1 pad.2.clone
  0.1 0.8 add_add_fusion.1
  0.8 0.1 add.72
  0.9 0.5 broadcast.61
  1.4 1.3 %reduce.3 = s32[4,10]{1,0:T(4,128)S(1)} reduce(s32[1,4,10,1]{2,3,1,0:T(1,128)} %param.5, s32[]{:T(128)} %broadcast.61), dimensions={0,3}, to_apply=%param.5.reduce_sub_computation.3 | reduce | bytes 324 | tf_op args[2]
  2.8 0.1 reshape.60
  2.9 0.2 convert_reduce_fusion
  3.1 0.1 select_reduce_fusion.1
  3.2 0.8 copy.4
  3.9 0.1 select_reduce_fusion
  4.1 0.1 add.65
  4.2 0.1 add_add_fusion.meta_ref
  4.2 0.0 copy-start
  4.2 1.3 %copy-done = bf16[4,20,64,64]{3,2,1,0:T(8,128)(2,1)S(1)} copy-done((bf16[4,20,64,64]{3,2,1,0:T(8,128)(2,1)S(1)}, bf16[4,20,64,64]{3,2,1,0:T(8,128)(2,1)}, u32[]{:S(2)}) %copy-start) | copy-done | bytes 655384
  5.5 38.4 %shard_map.37 = (bf16[8,1344,256]{2,1,0:T(8,128)(2,1)S(1)}, s32[8,8,128]{2,1,0:T(8,128)S(1)}) custom-call(bf16[4,20,64,64]{3,2,1,0:T(8,128)(2,1)S(1)} %copy-done, s32[8,128]{1,0:T(8,128)S(1)} %add_add_fusion.meta_ref), custom_call_target="tpu_custom_call" | custom-call | tf_op jit(solution)/shard_map/pallas_call | solution.py:317
  44.0 45.0 %shard_map.38 = bf16[8,16,64,64]{3,2,1,0:T(8,128)(2,1)} custom-call(bf16[8,1344,256]{2,1,0:T(8,128)(2,1)S(1)} %get-tuple-element.7.packed, s32[8,8,128]{2,1,0:T(8,128)S(1)} %get-tuple-element.8.meta_s), custom_call_target="tpu_custom_call" | custom-call | tf_op jit(solution)/shard_map/pallas_call | solution.py:336
  (6 shorter events, 0.0 us)
Async XLA Ops:
  4.2 1.3 %copy-start = (bf16[4,20,64,64]{3,2,1,0:T(8,128)(2,1)S(1)}, bf16[4,20,64,64]{3,2,1,0:T(8,128)(2,1)}, u32[]{:S(2)}) copy-start(bf16[4,20,64,64]{3,2,1,0:T(8,128)(2,1)} %blocks_ref.1) | copy-start | bytes 1966084

commit v2 on v1

--- a/solution.py
+++ b/solution.py
@@ -220,6 +220,19 @@
             copy(position, k, target, landed).wait_send()
 
 
+def chunk_product(devices, part, left_ref, right_ref, source, d):
+    def chunk(r):
+        return pl.ds(pl.multiple_of(lax.rem(source + r + devices, devices) * part, part), part)
+
+    def apart(r):
+        return min(r % devices, -r % devices)
+
+    between = [r for r in range(-HOPS, HOPS + 1) if apart(r - d) <= HOPS]
+    left = jnp.concatenate([left_ref[chunk(0), chunk(r)] for r in between], axis=1)
+    right = jnp.concatenate([right_ref[chunk(r), chunk(d)] for r in between], axis=0)
+    return chunk(0), chunk(d), jnp.dot(left, right, preferred_element_type=jnp.float32)
+
+
 def dense_kernel(dims, packed, meta_s, out_ref, x_ref, sq_ref, mask_ref, up_ref):
     n_row, n_col, rows, slots, size, capacity = dims
     devices = n_row * n_col
@@ -251,28 +264,24 @@
     lax.fori_loop(0, devices, expand, 0)
 
     inv_scale = 1.0 / math.sqrt(size * slots)
-    tile = 4 * 2 * size
 
     def square(source, carry):
-        own = pl.ds(pl.multiple_of(source * part, part), part)
-        for column in range(width // tile):
-            spot = slice(column * tile, (column + 1) * tile)
-            value = jnp.dot(x_ref[own, :], x_ref[:, spot], preferred_element_type=jnp.float32)
-            kept = jnp.broadcast_to(mask_ref[source, :, spot][:, None, :], (rows, size, tile))
-            sq_ref[own, spot] = (value * inv_scale * kept.reshape(part, tile)).astype(jnp.bfloat16)
+        for d in range(-HOPS, HOPS + 1):
+            own, spot, value = chunk_product(devices, part, x_ref, x_ref, source, d)
+            kept = jnp.broadcast_to(mask_ref[source, :, spot][:, None, :], (rows, size, part))
+            sq_ref[own, spot] = (value * inv_scale * kept.reshape(part, part)).astype(jnp.bfloat16)
         return carry
 
     lax.fori_loop(0, devices, square, 0)
 
     def cube(source, carry):
-        own = pl.ds(pl.multiple_of(source * part, part), part)
-        for column in range(width // tile):
-            spot = slice(column * tile, (column + 1) * tile)
-            value = jnp.dot(x_ref[own, :], sq_ref[:, spot], preferred_element_type=jnp.float32)
+        for d in range(-HOPS, HOPS + 1):
+            own, spot, value = chunk_product(devices, part, x_ref, sq_ref, source, d)
             value = 1.5 * x_ref[own, spot].astype(jnp.float32) - (0.5 * inv_scale) * value
             value = value.astype(jnp.bfloat16)
-            for t in range(4):
-                up_ref[column * 4 + t] = value[:, t * 2 * size : (t + 1) * 2 * size]
+            column = lax.rem(source + d + devices, devices)
+            for t in range(rows // 2):
+                up_ref[column * (rows // 2) + t] = value[:, t * 2 * size : (t + 1) * 2 * size]
         for rank in range(capacity):
             code = meta_s[source, 1, me * capacity + rank]
             found = jnp.maximum(code, 0)
@@ -355,7 +364,7 @@
         P(("groups", "row", "col"), None),
         P("depth", ("groups", "row", "col"), None, None),
     )
-    small = mesh.shape["row"] * mesh.shape["col"] <= 8 and mesh.shape["col"] == 2
+    small = mesh.shape["row"] * mesh.shape["col"] == 8 and mesh.shape["col"] == 2
     return jax.shard_map(
         dense_shards if small else shards,
         mesh=mesh,

time: 89.2 us -> 78.9 us (0.88)
  Pallas kernels: 83.4 us -> 73.1 us
    pallas_call x1, Pallas kernels: 45 us -> 34.7 us  [dense_shards(): pl.pallas_call(functools.partial(dense_kernel, dims), out_shape=jax.Shape...]
where the time goes in v2:
time: 78.9 us; the launch traced here: 78.7 us
  Pallas kernels  73.1 us (93%)
  local copies, waits for them, and re-layouts  2.94 us (4%)
  other arithmetic  2.58 us (3%)
    pallas_call x1, Pallas kernels, dense_shards(): pl.pallas_call(functools.partial(gather_kernel, dims), out_shape=(jax.Sha...  38.4 us
    pallas_call x1, Pallas kernels, dense_shards(): pl.pallas_call(functools.partial(dense_kernel, dims), out_shape=jax.Shape...  34.7 us
    unnamed x4, local copies, waits for them, and re-layouts  2.61 us

profile of v2, /device:TPU:0, one launch (start us, length us, event | category | flops | bytes accessed | tf_op | source)
XLA Modules:
  0.0 78.7 jit_solution(1632222266120872424)
XLA Ops:
  0.0 0.1 pad.2.clone
  0.1 0.8 add_add_fusion.1
  0.8 0.1 add.72
  0.9 0.5 broadcast.61
  1.4 1.3 %reduce.3 = s32[4,10]{1,0:T(4,128)S(1)} reduce(s32[1,4,10,1]{2,3,1,0:T(1,128)} %param.5, s32[]{:T(128)} %broadcast.61), dimensions={0,3}, to_apply=%param.5.reduce_sub_computation.3 | reduce | bytes 324 | tf_op args[2]
  2.8 0.1 reshape.60
  2.9 0.2 convert_reduce_fusion
  3.1 0.1 select_reduce_fusion.1
  3.2 0.8 copy.4
  3.9 0.1 select_reduce_fusion
  4.1 0.1 add.65
  4.2 0.1 add_add_fusion.meta_ref
  4.2 0.0 copy-start
  4.2 1.3 %copy-done = bf16[4,20,64,64]{3,2,1,0:T(8,128)(2,1)S(1)} copy-done((bf16[4,20,64,64]{3,2,1,0:T(8,128)(2,1)S(1)}, bf16[4,20,64,64]{3,2,1,0:T(8,128)(2,1)}, u32[]{:S(2)}) %copy-start) | copy-done | bytes 655384
  5.5 38.4 %shard_map.37 = (bf16[8,1344,256]{2,1,0:T(8,128)(2,1)S(1)}, s32[8,8,128]{2,1,0:T(8,128)S(1)}) custom-call(bf16[4,20,64,64]{3,2,1,0:T(8,128)(2,1)S(1)} %copy-done, s32[8,128]{1,0:T(8,128)S(1)} %add_add_fusion.meta_ref), custom_call_target="tpu_custom_call" | custom-call | tf_op jit(solution)/shard_map/pallas_call | solution.py:326
  44.0 34.7 %shard_map.38 = bf16[8,16,64,64]{3,2,1,0:T(8,128)(2,1)} custom-call(bf16[8,1344,256]{2,1,0:T(8,128)(2,1)S(1)} %get-tuple-element.7.packed, s32[8,8,128]{2,1,0:T(8,128)S(1)} %get-tuple-element.8.meta_s), custom_call_target="tpu_custom_call" | custom-call | tf_op jit(solution)/shard_map/pallas_call | solution.py:345
  (6 shorter events, 0.0 us)
Async XLA Ops:
  4.2 1.3 %copy-start = (bf16[4,20,64,64]{3,2,1,0:T(8,128)(2,1)S(1)}, bf16[4,20,64,64]{3,2,1,0:T(8,128)(2,1)}, u32[]{:S(2)}) copy-start(bf16[4,20,64,64]{3,2,1,0:T(8,128)(2,1)} %blocks_ref.1) | copy-start | bytes 1966084

commit v3 on v1

--- a/solution.py
+++ b/solution.py
@@ -110,13 +110,15 @@
 
 
 def gather_kernel(
-    dims, blocks_ref, meta_ref, packed, meta_v,
-    send_sem, recv_sem, sib_sem, meta_send, meta_recv,
+    dims, blocks_ref, meta_ref, x_ref, sq_ref, meta_v,
+    packed, meta_s, mask_ref,
+    send_sem, recv_sem, sib_sem, meta_send, meta_recv, local_sem, sq_send, sq_recv,
 ):
     n_row, n_col, rows, slots, size, capacity = dims
     devices = n_row * n_col
+    total = devices * rows
     part = rows * size
-    half_rows = slots // 2 * size
+    half_slots = slots // 2
     z, x, h = lax.axis_index("row"), lax.axis_index("col"), lax.axis_index("depth")
     me = z * n_col + x
     across = n_col - 1 - x
@@ -136,11 +138,11 @@
     pl.semaphore_signal(barrier, inc=1, device_id=sibling, device_id_type=MESH)
 
     for pair in range(rows // 2):
-        packed[me, : slots * size, pair * 2 * size : (pair + 1) * 2 * size] = jnp.concatenate(
-            [blocks_ref[2 * pair + t].reshape(slots * size, size) for t in range(2)], axis=1
+        packed[me, :slots, :, pair * 2 * size : (pair + 1) * 2 * size] = jnp.concatenate(
+            [blocks_ref[2 * pair + t] for t in range(2)], axis=2
         )
     for source in range(devices):
-        packed[source, slots * size :, :] = jnp.zeros((size, part), jnp.bfloat16)
+        packed[source, slots] = jnp.zeros((size, part), jnp.bfloat16)
     meta_v[me] = meta_ref[...]
     pl.semaphore_wait(barrier, devices)
 
@@ -153,7 +155,7 @@
         )
 
     def piece(position, which):
-        return packed.at[position, pl.ds(which * half_rows, half_rows), :]
+        return packed.at[position, pl.ds(which * half_slots, half_slots)]
 
     def copy(position, k, target, landed, which=None):
         ref = piece(position, h if which is None else which)
@@ -211,6 +213,9 @@
 
     for step in range(1, devices):
         meta_copy(step).wait()
+    local = pltpu.make_async_copy(meta_v, meta_s, local_sem)
+    local.start()
+    local.wait()
     for step in range(1, devices):
         position = lax.rem(me + step, devices)
         copy(position, 0, sibling, sib_sem, 1 - h).wait_recv()
@@ -219,15 +224,6 @@
         def _(position=position, k=k, target=target, landed=landed):
             copy(position, k, target, landed).wait_send()
 
-
-def dense_kernel(dims, packed, meta_s, out_ref, x_ref, sq_ref, mask_ref, up_ref):
-    n_row, n_col, rows, slots, size, capacity = dims
-    devices = n_row * n_col
-    total = devices * rows
-    width = total * size
-    part = rows * size
-    me = lax.axis_index("row") * n_col + lax.axis_index("col")
-
     lane = lax.broadcasted_iota(jnp.int32, (1, 2 * size), 1)
 
     def expand(source, carry):
@@ -237,7 +233,7 @@
             for pair in range(total // 2):
                 slot = [meta_s[source, 0, row * total + 2 * pair + t] for t in range(2)]
                 both = [
-                    packed[source, pl.ds(pl.multiple_of(slot[t] * size, size), size), lanes : lanes + 2 * size]
+                    packed[source, slot[t], :, lanes : lanes + 2 * size]
                     for t in range(2)
                 ]
                 spot = slice(pair * 2 * size, (pair + 1) * 2 * size)
@@ -251,28 +247,63 @@
     lax.fori_loop(0, devices, expand, 0)
 
     inv_scale = 1.0 / math.sqrt(size * slots)
-    tile = 4 * 2 * size
-
-    def square(source, carry):
-        own = pl.ds(pl.multiple_of(source * part, part), part)
-        for column in range(width // tile):
-            spot = slice(column * tile, (column + 1) * tile)
-            value = jnp.dot(x_ref[own, :], x_ref[:, spot], preferred_element_type=jnp.float32)
-            kept = jnp.broadcast_to(mask_ref[source, :, spot][:, None, :], (rows, size, tile))
-            sq_ref[own, spot] = (value * inv_scale * kept.reshape(part, tile)).astype(jnp.bfloat16)
+    share = devices // 2
+
+    def half_copy(side, step):
+        ref = sq_ref.at[pl.ds((side * share + step) * part, part), :]
+        return pltpu.make_async_remote_copy(
+            src_ref=ref, dst_ref=ref, send_sem=sq_send.at[step], recv_sem=sq_recv.at[step],
+            device_id=sibling, device_id_type=MESH,
+        )
+
+    def square(step, carry):
+        source = h * share + step
+        for d in range(-HOPS, HOPS + 1):
+            own, spot, value = chunk_product(devices, part, x_ref, x_ref, source, d)
+            kept = jnp.broadcast_to(mask_ref[source, :, spot][:, None, :], (rows, size, part))
+            sq_ref[own, spot] = (value * inv_scale * kept.reshape(part, part)).astype(jnp.bfloat16)
+        far = pl.ds(pl.multiple_of(lax.rem(source + HOPS + 1, devices) * part, part), part)
+        sq_ref[own, far] = jnp.zeros((part, part), jnp.bfloat16)
+        half_copy(h, step).start()
         return carry
 
-    lax.fori_loop(0, devices, square, 0)
+    lax.fori_loop(0, share, square, 0)
+    for step in range(share):
+        half_copy(h, step).wait_send()
+        half_copy(1 - h, step).wait_recv()
+
+
+def chunk_product(devices, part, left_ref, right_ref, source, d):
+    def chunk(r):
+        return pl.ds(pl.multiple_of(lax.rem(source + r + devices, devices) * part, part), part)
+
+    def apart(r):
+        return min(r % devices, -r % devices)
+
+    between = [r for r in range(-HOPS, HOPS + 1) if apart(r - d) <= HOPS]
+    left = jnp.concatenate([left_ref[chunk(0), chunk(r)] for r in between], axis=1)
+    right = jnp.concatenate([right_ref[chunk(r), chunk(d)] for r in between], axis=0)
+    return chunk(0), chunk(d), jnp.dot(left, right, preferred_element_type=jnp.float32)
+
+
+def dense_kernel(dims, x_ref, sq_ref, meta_s, out_ref, up_ref):
+    n_row, n_col, rows, slots, size, capacity = dims
+    devices = n_row * n_col
+    total = devices * rows
+    width = total * size
+    part = rows * size
+    me = lax.axis_index("row") * n_col + lax.axis_index("col")
+
+    inv_scale = 1.0 / math.sqrt(size * slots)
 
     def cube(source, carry):
-        own = pl.ds(pl.multiple_of(source * part, part), part)
-        for column in range(width // tile):
-            spot = slice(column * tile, (column + 1) * tile)
-            value = jnp.dot(x_ref[own, :], sq_ref[:, spot], preferred_element_type=jnp.float32)
+        for d in range(-HOPS, HOPS + 1):
+            own, spot, value = chunk_product(devices, part, x_ref, sq_ref, source, d)
             value = 1.5 * x_ref[own, spot].astype(jnp.float32) - (0.5 * inv_scale) * value
             value = value.astype(jnp.bfloat16)
-            for t in range(4):
-                up_ref[column * 4 + t] = value[:, t * 2 * size : (t + 1) * 2 * size]
+            column = lax.rem(source + d + devices, devices)
+            for t in range(rows // 2):
+                up_ref[column * (rows // 2) + t] = value[:, t * 2 * size : (t + 1) * 2 * size]
         for rank in range(capacity):
             code = meta_s[source, 1, me * capacity + rank]
             found = jnp.maximum(code, 0)
@@ -314,38 +345,40 @@
     dims = (n_row, n_col, rows, slots, size, capacity)
     width = total * size
     vmem = pl.BlockSpec(memory_space=pltpu.VMEM)
-    gathered, gathered_meta = pl.pallas_call(
+    dense, squared, gathered_meta = pl.pallas_call(
         functools.partial(gather_kernel, dims),
         out_shape=(
-            jax.ShapeDtypeStruct((devices, (slots + 1) * size, rows * size), jnp.bfloat16),
+            jax.ShapeDtypeStruct((width, width), jnp.bfloat16),
+            jax.ShapeDtypeStruct((width, width), jnp.bfloat16),
             jax.ShapeDtypeStruct((devices, 8, lanes), jnp.int32),
         ),
         in_specs=[vmem, vmem],
-        out_specs=(vmem, vmem),
+        out_specs=(vmem, vmem, vmem),
         scratch_shapes=[
+            pltpu.VMEM((devices, slots + 1, size, rows * size), jnp.bfloat16),
+            pltpu.SMEM((devices, 8, lanes), jnp.int32),
+            pltpu.VMEM((devices, rows, width), jnp.float32),
             pltpu.SemaphoreType.DMA((devices, 3)),
             pltpu.SemaphoreType.DMA((devices,)),
             pltpu.SemaphoreType.DMA((devices,)),
             pltpu.SemaphoreType.DMA((devices,)),
             pltpu.SemaphoreType.DMA((devices,)),
+            pltpu.SemaphoreType.DMA,
+            pltpu.SemaphoreType.DMA((devices // 2,)),
+            pltpu.SemaphoreType.DMA((devices // 2,)),
         ],
         compiler_params=pltpu.CompilerParams(
-            collective_id=0, has_side_effects=True, vmem_limit_bytes=24 * 1024 * 1024
+            collective_id=0, has_side_effects=True, vmem_limit_bytes=32 * 1024 * 1024
         ),
     )(blocks, meta)
     out = pl.pallas_call(
         functools.partial(dense_kernel, dims),
         out_shape=jax.ShapeDtypeStruct((devices, capacity, size, size), jnp.bfloat16),
-        in_specs=[vmem, pl.BlockSpec(memory_space=pltpu.SMEM)],
+        in_specs=[vmem, vmem, pl.BlockSpec(memory_space=pltpu.SMEM)],
         out_specs=vmem,
-        scratch_shapes=[
-            pltpu.VMEM((width, width), jnp.bfloat16),
-            pltpu.VMEM((width, width), jnp.bfloat16),
-            pltpu.VMEM((devices, rows, width), jnp.float32),
-            pltpu.VMEM((total // 2, rows * size, 2 * size), jnp.bfloat16),
-        ],
-        compiler_params=pltpu.CompilerParams(vmem_limit_bytes=40 * 1024 * 1024),
-    )(gathered, gathered_meta)
+        scratch_shapes=[pltpu.VMEM((total // 2, rows * size, 2 * size), jnp.bfloat16)],
+        compiler_params=pltpu.CompilerParams(vmem_limit_bytes=28 * 1024 * 1024),
+    )(dense, squared, gathered_meta)
     return out.reshape(1, 1, devices, capacity, size, size)
 
 
@@ -355,7 +388,7 @@
         P(("groups", "row", "col"), None),
         P("depth", ("groups", "row", "col"), None, None),
     )
-    small = mesh.shape["row"] * mesh.shape["col"] <= 8 and mesh.shape["col"] == 2
+    small = mesh.shape["row"] * mesh.shape["col"] == 8 and mesh.shape["col"] == 2
     return jax.shard_map(
         dense_shards if small else shards,
         mesh=mesh,

time: 89.2 us -> 74.2 us (0.83)
  Pallas kernels: 83.4 us -> 68.4 us
    pallas_call x1, Pallas kernels: 45 us -> 17.3 us  [dense_shards(): pl.pallas_call(functools.partial(dense_kernel, dims), out_shape=jax.Shape...]
    pallas_call x1, Pallas kernels: 38.4 us -> 51.1 us  [dense_shards(): pl.pallas_call(functools.partial(gather_kernel, dims), out_shape=(jax.Sha...]
where the time goes in v3:
time: 74.2 us; the launch traced here: 74 us
  Pallas kernels  68.4 us (92%)
  local copies, waits for them, and re-layouts  2.94 us (4%)
  other arithmetic  2.58 us (3%)
    pallas_call x1, Pallas kernels, dense_shards(): pl.pallas_call(functools.partial(gather_kernel, dims), out_shape=(jax.Sha...  51.1 us
    pallas_call x1, Pallas kernels, dense_shards(): pl.pallas_call(functools.partial(dense_kernel, dims), out_shape=jax.Shape...  17.3 us
    unnamed x4, local copies, waits for them, and re-layouts  2.61 us

profile of v3, /device:TPU:0, one launch (start us, length us, event | category | flops | bytes accessed | tf_op | source)
XLA Modules:
  0.0 74.0 jit_solution(13290969580291810503)
XLA Ops:
  0.0 0.1 pad.2.clone
  0.1 0.8 %add_add_fusion.1 = s32[4,10]{1,0:T(4,128)S(1)} fusion(s32[4,20]{1,0:T(4,128)} %param.4, s32[]{:T(128)S(6)} %select_n.12, s32[4]{0:T(128)S(1)} %iota_multiply_fusion), kind=kLoop, calls=%fused_computation.8 | loop fusion | flops 80 | bytes 340 | tf_op jit(solution)/shard_map/add | solution.py:340
  0.8 0.1 add.72
  0.9 0.5 broadcast.61
  1.4 1.3 %reduce.3 = s32[4,10]{1,0:T(4,128)S(1)} reduce(s32[1,4,10,1]{2,3,1,0:T(1,128)} %param.5, s32[]{:T(128)} %broadcast.61), dimensions={0,3}, to_apply=%param.5.reduce_sub_computation.3 | reduce | bytes 324 | tf_op args[2]
  2.8 0.1 reshape.60
  2.9 0.2 convert_reduce_fusion
  3.1 0.1 select_reduce_fusion.1
  3.2 0.8 %copy.4 = s32[4,20]{0,1:T(8,128)S(1)} copy(s32[4,20]{1,0:T(4,128)} %param.4) | data formatting | bytes 640 | tf_op args[1]
  3.9 0.1 select_reduce_fusion
  4.1 0.1 add.65
  4.2 0.1 add_add_fusion.meta_ref
  4.2 0.0 copy-start
  4.2 1.3 %copy-done = bf16[4,20,64,64]{3,2,1,0:T(8,128)(2,1)S(1)} copy-done((bf16[4,20,64,64]{3,2,1,0:T(8,128)(2,1)S(1)}, bf16[4,20,64,64]{3,2,1,0:T(8,128)(2,1)}, u32[]{:S(2)}) %copy-start) | copy-done | bytes 655384
  5.5 51.1 %shard_map.37 = (bf16[2048,2048]{1,0:T(8,128)(2,1)S(1)}, bf16[2048,2048]{1,0:T(8,128)(2,1)S(1)}, s32[8,8,128]{2,1,0:T(8,128)S(1)}) custom-call(bf16[4,20,64,64]{3,2,1,0:T(8,128)(2,1)S(1)} %copy-done, s32[8,128]{1,0:T(8,128)S(1)} %add_add_fusion.meta_ref), custom_call_target="tpu_custom_call" | custom-call | tf_op jit(solution)/shard_map/pallas_call | solution.py:348
  56.7 17.3 %shard_map.38 = bf16[8,16,64,64]{3,2,1,0:T(8,128)(2,1)} custom-call(bf16[2048,2048]{1,0:T(8,128)(2,1)S(1)} %get-tuple-element.8.x_ref, bf16[2048,2048]{1,0:T(8,128)(2,1)S(1)} %get-tuple-element.9.sq_ref, s32[8,8,128]{2,1,0:T(8,128)S(1)} %get-tuple-element.10.meta_s), custom_call_target="tpu_custom_call" | custom-call | tf_op jit(solution)/shard_map/pallas_call | solution.py:374
  (6 shorter events, 0.0 us)
Async XLA Ops:
  4.2 1.3 %copy-start = (bf16[4,20,64,64]{3,2,1,0:T(8,128)(2,1)S(1)}, bf16[4,20,64,64]{3,2,1,0:T(8,128)(2,1)}, u32[]{:S(2)}) copy-start(bf16[4,20,64,64]{3,2,1,0:T(8,128)(2,1)} %blocks_ref.1) | copy-start | bytes 1966084

commit v4 on v3

--- a/solution.py
+++ b/solution.py
@@ -110,14 +110,15 @@
 
 
 def gather_kernel(
-    dims, blocks_ref, meta_ref, x_ref, sq_ref, meta_v,
-    packed, meta_s, mask_ref,
-    send_sem, recv_sem, sib_sem, meta_send, meta_recv, local_sem, sq_send, sq_recv,
+    dims, blocks_hbm, pattern_ref, owner_ref, x_ref, sq_ref, meta_v,
+    blocks_ref, packed, meta_s, mask_ref,
+    send_sem, recv_sem, sib_sem, meta_send, meta_recv, local_sem, sq_send, sq_recv, load_sem,
 ):
     n_row, n_col, rows, slots, size, capacity = dims
     devices = n_row * n_col
     total = devices * rows
     part = rows * size
+    lanes = meta_v.shape[2]
     half_slots = slots // 2
     z, x, h = lax.axis_index("row"), lax.axis_index("col"), lax.axis_index("depth")
     me = z * n_col + x
@@ -127,6 +128,8 @@
         return {"row": to_z, "col": to_x, "depth": to_h}
 
     sibling = device(z, x, 1 - h)
+    load = pltpu.make_async_copy(blocks_hbm, blocks_ref, load_sem)
+    load.start()
 
     barrier = pltpu.get_barrier_semaphore()
     for step in range(1, devices):
@@ -137,13 +140,13 @@
         )
     pl.semaphore_signal(barrier, inc=1, device_id=sibling, device_id_type=MESH)
 
+    for source in range(devices):
+        packed[source, slots] = jnp.zeros((size, part), jnp.bfloat16)
+    load.wait()
     for pair in range(rows // 2):
         packed[me, :slots, :, pair * 2 * size : (pair + 1) * 2 * size] = jnp.concatenate(
             [blocks_ref[2 * pair + t] for t in range(2)], axis=2
         )
-    for source in range(devices):
-        packed[source, slots] = jnp.zeros((size, part), jnp.bfloat16)
-    meta_v[me] = meta_ref[...]
     pl.semaphore_wait(barrier, devices)
 
     def meta_copy(step):
@@ -172,11 +175,31 @@
             copy(position, k, target, landed).start()
         sends.append((valid, position, k, target, landed))
 
-    for step in range(1, devices):
-        meta_copy(step).start()
     start(z > 0, me, 0, device(z - 1, x, h), recv_sem)
     start(z < n_row - 1, me, 1, device(z + 1, x, h), recv_sem)
     start(z >= 0, me, 2, device(z, across, h), recv_sem)
+
+    lane_number = lax.broadcasted_iota(jnp.int32, (rows, lanes), 1)
+    slot_of = jnp.full((rows, lanes), slots, jnp.int32)
+    for slot in range(slots):
+        slot_of = jnp.where(pattern_ref[:, slot : slot + 1] == lane_number, slot, slot_of)
+    meta_v[me, :rows, :] = slot_of
+    meta_v[me, rows:8, :] = jnp.full((8 - rows, lanes), slots, jnp.int32)
+    rank_number = lax.broadcasted_iota(jnp.int32, (devices, lanes), 1)
+    owner_number = lax.broadcasted_iota(jnp.int32, (devices, lanes), 0)
+    item_at = jnp.full((devices, lanes), -1, jnp.int32)
+    count = jnp.zeros((devices, lanes), jnp.int32)
+    for row in range(rows):
+        for slot in range(half_slots):
+            named = owner_number == owner_ref[row, :, slot : slot + 1]
+            low = pattern_ref[row : row + 1, slot : slot + 1]
+            high = pattern_ref[row : row + 1, half_slots + slot : half_slots + slot + 1]
+            code = row * total + low + (high - low) * h
+            item_at = jnp.where(named & (rank_number == count), code, item_at)
+            count = count + named.astype(jnp.int32)
+    meta_v[me, 8:, :] = item_at
+    for step in range(1, devices):
+        meta_copy(step).start()
 
     def from_z(distance, way):
         source = z + way * distance
@@ -231,7 +254,7 @@
             lanes = row // 2 * 2 * size
             at = row % 2 * size
             for pair in range(total // 2):
-                slot = [meta_s[source, 0, row * total + 2 * pair + t] for t in range(2)]
+                slot = [meta_s[source, row, 2 * pair + t] for t in range(2)]
                 both = [
                     packed[source, slot[t], :, lanes : lanes + 2 * size]
                     for t in range(2)
@@ -305,7 +328,7 @@
             for t in range(rows // 2):
                 up_ref[column * (rows // 2) + t] = value[:, t * 2 * size : (t + 1) * 2 * size]
         for rank in range(capacity):
-            code = meta_s[source, 1, me * capacity + rank]
+            code = meta_s[source, 8 + me, rank]
             found = jnp.maximum(code, 0)
             column = found & (total - 1)
             row = found >> (total.bit_length() - 1)
@@ -325,23 +348,7 @@
     total = devices * rows
     items = rows * (slots // 2)
     capacity = max(2, 3 * items // devices + 1)
-    h = lax.axis_index("depth")
-
-    slot_number = jnp.arange(slots, dtype=jnp.int32)[None, :, None]
-    named = pattern[:, :, None] == jnp.arange(total, dtype=jnp.int32)[None, None, :]
-    slot_of = slots + jnp.sum(jnp.where(named, slot_number - slots, 0), axis=1)
-
-    targets = owner_map.reshape(items)
-    earlier = jnp.arange(items)[:, None] > jnp.arange(items)[None, :]
-    rank = jnp.sum(((targets[:, None] == targets[None, :]) & earlier).astype(jnp.int32), axis=1)
-    columns = lax.dynamic_slice_in_dim(pattern, h * (slots // 2), slots // 2, 1)
-    code = jnp.arange(rows, dtype=jnp.int32)[:, None] * total + columns
-    placed = jnp.arange(devices * capacity, dtype=jnp.int32)[:, None] == (targets * capacity + rank)[None, :]
-    item_at = jnp.sum(jnp.where(placed, code.reshape(1, items) + 1, 0), axis=1) - 1
     lanes = 128
-    meta = jnp.concatenate(
-        [slot_of.reshape(1, lanes), item_at.reshape(1, lanes), jnp.zeros((6, lanes), jnp.int32)], axis=0
-    )
     dims = (n_row, n_col, rows, slots, size, capacity)
     width = total * size
     vmem = pl.BlockSpec(memory_space=pltpu.VMEM)
@@ -350,13 +357,14 @@
         out_shape=(
             jax.ShapeDtypeStruct((width, width), jnp.bfloat16),
             jax.ShapeDtypeStruct((width, width), jnp.bfloat16),
-            jax.ShapeDtypeStruct((devices, 8, lanes), jnp.int32),
+            jax.ShapeDtypeStruct((devices, 16, lanes), jnp.int32),
         ),
-        in_specs=[vmem, vmem],
+        in_specs=[pl.BlockSpec(memory_space=pltpu.HBM), vmem, vmem],
         out_specs=(vmem, vmem, vmem),
         scratch_shapes=[
+            pltpu.VMEM(blocks.shape, jnp.bfloat16),
             pltpu.VMEM((devices, slots + 1, size, rows * size), jnp.bfloat16),
-            pltpu.SMEM((devices, 8, lanes), jnp.int32),
+            pltpu.SMEM((devices, 16, lanes), jnp.int32),
             pltpu.VMEM((devices, rows, width), jnp.float32),
             pltpu.SemaphoreType.DMA((devices, 3)),
             pltpu.SemaphoreType.DMA((devices,)),
@@ -366,11 +374,12 @@
             pltpu.SemaphoreType.DMA,
             pltpu.SemaphoreType.DMA((devices // 2,)),
             pltpu.SemaphoreType.DMA((devices // 2,)),
+            pltpu.SemaphoreType.DMA,
         ],
         compiler_params=pltpu.CompilerParams(
             collective_id=0, has_side_effects=True, vmem_limit_bytes=32 * 1024 * 1024
         ),
-    )(blocks, meta)
+    )(blocks, pattern, owner_map.reshape(rows, 1, slots // 2))
     out = pl.pallas_call(
         functools.partial(dense_kernel, dims),
         out_shape=jax.ShapeDtypeStruct((devices, capacity, size, size), jnp.bfloat16),

time: 74.2 us -> 71.4 us (0.962)
  other arithmetic: 2.58 us -> 0 us
    unnamed x1 -> x0, other arithmetic: 1.34 us -> none
    add x3 -> x0, other arithmetic: 0.76 us -> none  [the longest x1 0.75 us: dense_shards(): code.reshape(1, items) + 1]
    unnamed x4 -> x6, local copies, waits for them, and re-layouts: 2.61 us -> 2.68 us
where the time goes in v4:
time: 71.4 us; the launch traced here: 71.2 us
  Pallas kernels  68.5 us (96%)
  local copies, waits for them, and re-layouts  2.68 us (4%)
    pallas_call x1, Pallas kernels, dense_shards(): pl.pallas_call(functools.partial(gather_kernel, dims), out_shape=(jax.Sha...  50.6 us
    pallas_call x1, Pallas kernels, dense_shards(): pl.pallas_call(functools.partial(dense_kernel, dims), out_shape=jax.Shape...  17.9 us
    unnamed x6, local copies, waits for them, and re-layouts  2.68 us

profile of v4, /device:TPU:0, one launch (start us, length us, event | category | flops | bytes accessed | tf_op | source)
XLA Modules:
  0.0 71.2 jit_solution(8679497897659517377)
XLA Ops:
  0.0 0.0 copy-start
  0.0 1.3 %copy-done = bf16[4,20,64,64]{3,2,1,0:T(8,128)(2,1)S(1)} copy-done((bf16[4,20,64,64]{3,2,1,0:T(8,128)(2,1)S(1)}, bf16[4,20,64,64]{3,2,1,0:T(8,128)(2,1)}, u32[]{:S(2)}) %copy-start) | copy-done | bytes 655384
  1.3 0.0 copy-start.1
  1.3 0.7 copy-done.1
  2.0 0.0 copy-start.2
  2.0 0.7 copy-done.2
  2.7 50.6 %shard_map.37 = (bf16[2048,2048]{1,0:T(8,128)(2,1)S(1)}, bf16[2048,2048]{1,0:T(8,128)(2,1)S(1)}, s32[8,16,128]{2,1,0:T(8,128)S(1)}) custom-call(bf16[4,20,64,64]{3,2,1,0:T(8,128)(2,1)S(1)} %copy-done, s32[4,20]{1,0:T(4,128)S(1)} %copy-done.1, s32[4,1,10]{2,1,0:T(1,128)S(1)} %bitcast.4), custom_call_target="tpu_custom_call" | custom-call | tf_op jit(solution)/shard_map/pallas_call | solution.py:355
  53.3 17.9 %shard_map.38 = bf16[8,16,64,64]{3,2,1,0:T(8,128)(2,1)} custom-call(bf16[2048,2048]{1,0:T(8,128)(2,1)S(1)} %get-tuple-element.8.x_ref, bf16[2048,2048]{1,0:T(8,128)(2,1)S(1)} %get-tuple-element.9.sq_ref, s32[8,16,128]{2,1,0:T(8,128)S(1)} %get-tuple-element.10.meta_s), custom_call_target="tpu_custom_call" | custom-call | tf_op jit(solution)/shard_map/pallas_call | solution.py:383
Async XLA Ops:
  0.0 1.3 %copy-start = (bf16[4,20,64,64]{3,2,1,0:T(8,128)(2,1)S(1)}, bf16[4,20,64,64]{3,2,1,0:T(8,128)(2,1)}, u32[]{:S(2)}) copy-start(bf16[4,20,64,64]{3,2,1,0:T(8,128)(2,1)} %blocks_hbm.1) | copy-start | bytes 1966084
  1.3 0.7 copy-start.1
  2.0 0.7 copy-start.2

commit v5 on v4

--- a/solution.py
+++ b/solution.py
@@ -157,27 +157,30 @@
             device_id=device(peer // n_col, lax.rem(peer, n_col), h), device_id_type=MESH,
         )
 
-    def piece(position, which):
-        return packed.at[position, pl.ds(which * half_slots, half_slots)]
-
-    def copy(position, k, target, landed, which=None):
-        ref = piece(position, h if which is None else which)
+    bit = half_slots // 2
+
+    def piece(position, which, q):
+        return packed.at[position, pl.ds(which * half_slots + q * bit, bit)]
+
+    def copy(position, k, q, target, landed, which=None):
+        ref = piece(position, h if which is None else which, q)
         return pltpu.make_async_remote_copy(
-            src_ref=ref, dst_ref=ref, send_sem=send_sem.at[position, k],
-            recv_sem=landed.at[position], device_id=target, device_id_type=MESH,
+            src_ref=ref, dst_ref=ref, send_sem=send_sem.at[position, k, q],
+            recv_sem=landed.at[position, q], device_id=target, device_id_type=MESH,
         )
 
     sends = []
 
-    def start(valid, position, k, target, landed):
+    def start(valid, *what):
         @pl.when(valid)
         def _():
-            copy(position, k, target, landed).start()
-        sends.append((valid, position, k, target, landed))
-
-    start(z > 0, me, 0, device(z - 1, x, h), recv_sem)
-    start(z < n_row - 1, me, 1, device(z + 1, x, h), recv_sem)
-    start(z >= 0, me, 2, device(z, across, h), recv_sem)
+            copy(*what).start()
+        sends.append((valid, what))
+
+    for q in range(2):
+        start(z > 0, me, 0, q, device(z - 1, x, h), recv_sem)
+        start(z < n_row - 1, me, 1, q, device(z + 1, x, h), recv_sem)
+        start(z >= 0, me, 2, q, device(z, across, h), recv_sem)
 
     lane_number = lax.broadcasted_iota(jnp.int32, (rows, lanes), 1)
     slot_of = jnp.full((rows, lanes), slots, jnp.int32)
@@ -201,38 +204,38 @@
     for step in range(1, devices):
         meta_copy(step).start()
 
-    def from_z(distance, way):
+    def from_z(distance, way, q):
         source = z + way * distance
         valid = (source >= 0) & (source < n_row)
         position = source * n_col + x
 
         @pl.when(valid)
         def _():
-            copy(position, 0, sibling, recv_sem).wait_recv()
-        start(valid & (z - way >= 0) & (z - way < n_row), position, 0, device(z - way, x, h), recv_sem)
-        start(valid, position, 1, device(z, across, h), recv_sem)
-        start(valid, position, 2, sibling, sib_sem)
-
-    def from_x(distance, way):
+            copy(position, 0, q, sibling, recv_sem).wait_recv()
+        start(valid & (z - way >= 0) & (z - way < n_row), position, 0, q, device(z - way, x, h), recv_sem)
+        start(valid, position, 1, q, device(z, across, h), recv_sem)
+        start(valid, position, 2, q, sibling, sib_sem)
+
+    def from_x(distance, way, q):
         source = z + way * distance
         valid = (source >= 0) & (source < n_row)
         position = source * n_col + across
 
         @pl.when(valid)
         def _():
-            copy(position, 0, sibling, recv_sem).wait_recv()
-        start(valid, position, 0, sibling, sib_sem)
+            copy(position, 0, q, sibling, recv_sem).wait_recv()
+        start(valid, position, 0, q, sibling, sib_sem)
 
     for distance in range(1, n_row):
-        from_z(distance, 1)
-        from_z(distance, -1)
-        if distance == 1:
-            from_x(0, 1)
-        else:
-            from_x(distance - 1, 1)
-            from_x(distance - 1, -1)
-    from_x(n_row - 1, 1)
-    from_x(n_row - 1, -1)
+        for q in range(2):
+            from_z(distance, 1, q)
+            from_z(distance, -1, q)
+            from_x(distance - 1, 1, q)
+            if distance > 1:
+                from_x(distance - 1, -1, q)
+    for q in range(2):
+        from_x(n_row - 1, 1, q)
+        from_x(n_row - 1, -1, q)
 
     for step in range(1, devices):
         meta_copy(step).wait()
@@ -241,11 +244,12 @@
     local.wait()
     for step in range(1, devices):
         position = lax.rem(me + step, devices)
-        copy(position, 0, sibling, sib_sem, 1 - h).wait_recv()
-    for valid, position, k, target, landed in sends:
+        for q in range(2):
+            copy(position, 0, q, sibling, sib_sem, 1 - h).wait_recv()
+    for valid, what in sends:
         @pl.when(valid)
-        def _(position=position, k=k, target=target, landed=landed):
-            copy(position, k, target, landed).wait_send()
+        def _(what=what):
+            copy(*what).wait_send()
 
     lane = lax.broadcasted_iota(jnp.int32, (1, 2 * size), 1)
 
@@ -366,9 +370,9 @@
             pltpu.VMEM((devices, slots + 1, size, rows * size), jnp.bfloat16),
             pltpu.SMEM((devices, 16, lanes), jnp.int32),
             pltpu.VMEM((devices, rows, width), jnp.float32),
-            pltpu.SemaphoreType.DMA((devices, 3)),
-            pltpu.SemaphoreType.DMA((devices,)),
-            pltpu.SemaphoreType.DMA((devices,)),
+            pltpu.SemaphoreType.DMA((devices, 3, 2)),
+            pltpu.SemaphoreType.DMA((devices, 2)),
+            pltpu.SemaphoreType.DMA((devices, 2)),
             pltpu.SemaphoreType.DMA((devices,)),
             pltpu.SemaphoreType.DMA((devices,)),
             pltpu.SemaphoreType.DMA,

time: 71.4 us -> 71.7 us (level)
  no operation moved by 1% of the time
where the time goes in v5:
time: 71.7 us; the launch traced here: 71.5 us
  Pallas kernels  68.8 us (96%)
  local copies, waits for them, and re-layouts  2.68 us (4%)
    pallas_call x1, Pallas kernels, dense_shards(): pl.pallas_call(functools.partial(gather_kernel, dims), out_shape=(jax.Sha...  50.9 us
    pallas_call x1, Pallas kernels, dense_shards(): pl.pallas_call(functools.partial(dense_kernel, dims), out_shape=jax.Shape...  17.9 us
    unnamed x6, local copies, waits for them, and re-layouts  2.68 us

profile of v5, /device:TPU:0, one launch (start us, length us, event | category | flops | bytes accessed | tf_op | source)
XLA Modules:
  0.0 71.5 jit_solution(3327677698034359761)
XLA Ops:
  0.0 0.0 copy-start
  0.0 1.3 %copy-done = bf16[4,20,64,64]{3,2,1,0:T(8,128)(2,1)S(1)} copy-done((bf16[4,20,64,64]{3,2,1,0:T(8,128)(2,1)S(1)}, bf16[4,20,64,64]{3,2,1,0:T(8,128)(2,1)}, u32[]{:S(2)}) %copy-start) | copy-done | bytes 655384
  1.3 0.0 copy-start.1
  1.3 0.7 copy-done.1
  2.0 0.0 copy-start.2
  2.0 0.7 copy-done.2
  2.7 50.9 %shard_map.37 = (bf16[2048,2048]{1,0:T(8,128)(2,1)S(1)}, bf16[2048,2048]{1,0:T(8,128)(2,1)S(1)}, s32[8,16,128]{2,1,0:T(8,128)S(1)}) custom-call(bf16[4,20,64,64]{3,2,1,0:T(8,128)(2,1)S(1)} %copy-done, s32[4,20]{1,0:T(4,128)S(1)} %copy-done.1, s32[4,1,10]{2,1,0:T(1,128)S(1)} %bitcast.4), custom_call_target="tpu_custom_call" | custom-call | tf_op jit(solution)/shard_map/pallas_call | solution.py:359
  53.6 17.9 %shard_map.38 = bf16[8,16,64,64]{3,2,1,0:T(8,128)(2,1)} custom-call(bf16[2048,2048]{1,0:T(8,128)(2,1)S(1)} %get-tuple-element.8.x_ref, bf16[2048,2048]{1,0:T(8,128)(2,1)S(1)} %get-tuple-element.9.sq_ref, s32[8,16,128]{2,1,0:T(8,128)S(1)} %get-tuple-element.10.meta_s), custom_call_target="tpu_custom_call" | custom-call | tf_op jit(solution)/shard_map/pallas_call | solution.py:387
Async XLA Ops:
  0.0 1.3 %copy-start = (bf16[4,20,64,64]{3,2,1,0:T(8,128)(2,1)S(1)}, bf16[4,20,64,64]{3,2,1,0:T(8,128)(2,1)}, u32[]{:S(2)}) copy-start(bf16[4,20,64,64]{3,2,1,0:T(8,128)(2,1)} %blocks_hbm.1) | copy-start | bytes 1966084
  1.3 0.7 copy-start.1
  2.0 0.7 copy-start.2

commit v6 on v5

--- a/solution.py
+++ b/solution.py
@@ -213,7 +213,11 @@
         def _():
             copy(position, 0, q, sibling, recv_sem).wait_recv()
         start(valid & (z - way >= 0) & (z - way < n_row), position, 0, q, device(z - way, x, h), recv_sem)
-        start(valid, position, 1, q, device(z, across, h), recv_sem)
+        crossing = valid
+        if q == 1 and distance == 1:
+            crossing = valid & (source > 0) & (source < n_row - 1)
+        if q == 0 or distance < n_row - 1:
+            start(crossing, position, 1, q, device(z, across, h), recv_sem)
         start(valid, position, 2, q, sibling, sib_sem)
 
     def from_x(distance, way, q):
@@ -224,6 +228,11 @@
         @pl.when(valid)
         def _():
             copy(position, 0, q, sibling, recv_sem).wait_recv()
+        if q == 1 and distance in (0, n_row - 2):
+            up = valid & (source == 0) & (z == distance)
+            down = valid & (source == n_row - 1) & (z == n_row - 1 - distance)
+            start(up, position, 1, q, device(z + 1, x, h), recv_sem)
+            start(down, position, 1, q, device(z - 1, x, h), recv_sem)
         start(valid, position, 0, q, sibling, sib_sem)
 
     for distance in range(1, n_row):

time: 71.7 us -> 72.2 us (level)
  no operation moved by 1% of the time
where the time goes in v6:
time: 72.2 us; the launch traced here: 72 us
  Pallas kernels  69.3 us (96%)
  local copies, waits for them, and re-layouts  2.68 us (4%)
    pallas_call x1, Pallas kernels, dense_shards(): pl.pallas_call(functools.partial(gather_kernel, dims), out_shape=(jax.Sha...  51.4 us
    pallas_call x1, Pallas kernels, dense_shards(): pl.pallas_call(functools.partial(dense_kernel, dims), out_shape=jax.Shape...  17.9 us
    unnamed x6, local copies, waits for them, and re-layouts  2.68 us

profile of v6, /device:TPU:0, one launch (start us, length us, event | category | flops | bytes accessed | tf_op | source)
XLA Modules:
  0.0 72.0 jit_solution(14642788079275554462)
XLA Ops:
  0.0 0.0 copy-start
  0.0 1.3 %copy-done = bf16[4,20,64,64]{3,2,1,0:T(8,128)(2,1)S(1)} copy-done((bf16[4,20,64,64]{3,2,1,0:T(8,128)(2,1)S(1)}, bf16[4,20,64,64]{3,2,1,0:T(8,128)(2,1)}, u32[]{:S(2)}) %copy-start) | copy-done | bytes 655384
  1.3 0.0 copy-start.1
  1.3 0.7 copy-done.1
  2.0 0.0 copy-start.2
  2.0 0.7 copy-done.2
  2.7 51.4 %shard_map.37 = (bf16[2048,2048]{1,0:T(8,128)(2,1)S(1)}, bf16[2048,2048]{1,0:T(8,128)(2,1)S(1)}, s32[8,16,128]{2,1,0:T(8,128)S(1)}) custom-call(bf16[4,20,64,64]{3,2,1,0:T(8,128)(2,1)S(1)} %copy-done, s32[4,20]{1,0:T(4,128)S(1)} %copy-done.1, s32[4,1,10]{2,1,0:T(1,128)S(1)} %bitcast.4), custom_call_target="tpu_custom_call" | custom-call | tf_op jit(solution)/shard_map/pallas_call | solution.py:368
  54.1 17.9 %shard_map.38 = bf16[8,16,64,64]{3,2,1,0:T(8,128)(2,1)} custom-call(bf16[2048,2048]{1,0:T(8,128)(2,1)S(1)} %get-tuple-element.8.x_ref, bf16[2048,2048]{1,0:T(8,128)(2,1)S(1)} %get-tuple-element.9.sq_ref, s32[8,16,128]{2,1,0:T(8,128)S(1)} %get-tuple-element.10.meta_s), custom_call_target="tpu_custom_call" | custom-call | tf_op jit(solution)/shard_map/pallas_call | solution.py:396
Async XLA Ops:
  0.0 1.3 %copy-start = (bf16[4,20,64,64]{3,2,1,0:T(8,128)(2,1)S(1)}, bf16[4,20,64,64]{3,2,1,0:T(8,128)(2,1)}, u32[]{:S(2)}) copy-start(bf16[4,20,64,64]{3,2,1,0:T(8,128)(2,1)} %blocks_hbm.1) | copy-start | bytes 1966084
  1.3 0.7 copy-start.1
  2.0 0.7 copy-start.2
